TPU v7x, 32 devices: a whole 2x2x4 slice. The times are simulated.
32 devices in a mesh: group: 2 (over x), dom: 16 (over z, y, core).
Axes of the slice: x: 2, y: 2, z: 4, core: 2. Of those that a mesh axis runs over, the one named last changes fastest.
Arguments:
- fields: float32 [6, 35, 32768], P(None, None, ('group', 'dom')), may hold values from -6 to 6
- metric: float32 [9, 32768], P(None, ('group', 'dom')), may hold values from -3 to 3
- face_scale: float32 [4, 32768], P(None, ('group', 'dom')), may hold values from 0.5 to 10
- face_angles: float32 [2, 4, 32768], P(None, None, ('group', 'dom')), may hold values from -3.140625 to 3.140625
- neighbours: int32 [4, 32768], P(None, ('group', 'dom')), may hold values from -1 to 4479, as said below
- send_dom: int32 [2, 4096], P(None, ('group', 'dom')), may hold values from 0 to 4095, as said below
- send_partner: int32 [4096], P(('group', 'dom')), may hold values from 0 to 4095, as said below
- element_kind: int32 [32768], P(('group', 'dom')), may hold values from 0 to 6, as said below
- derivative: float32 [3, 35, 35], replicated, may hold values from -1 to 1
- lifting: float32 [35, 60], replicated, may hold values from -0.75 to 0.75
- block_inverse: bfloat16 [6, 210, 210], replicated
Outputs:
- advanced: float32 [6, 35, 32768], P(None, None, ('group', 'dom'))
Inputs may be any that keep to these rules, and one draw needn't show every extreme that they name: `send_dom`: values are local face ids f * 1024 + e. Row 0 lists exactly the faces of the device whose neighbours slots are 4096 + i for i < 128, in the order of i; row 1 those with 4224 + i, in the order of i. `send_partner`: values are local face ids; exactly the faces of the device whose neighbours slot is 4352 + i, in the order of i. `neighbours`: on each device: every slot from 4096 up is read by exactly one face; 128 faces hold -1; every other face holds the id of another face of the same device, and that face holds its id. `element_kind`: elements of kind 1 or more (the fine region) lie exactly on the devices with group index 1 and dom index at least half of the dom axis; all elements of those devices have kind 1 or more, all others kind 0.
All inputs are finite; a program needn't handle non-finite values.
Results may differ from a plain program's by a relative error of at most 0.0003.
Values sent between devices are 32-bit elements; how exact they have to be, the bound alone decides.
A program may use at most 64 MiB of HBM per device.

v0:
```python
import functools

import jax
import jax.numpy as jnp
import numpy as np
from jax import lax
from jax.experimental import pallas as pl
from jax.experimental.pallas import tpu as pltpu
from jax.sharding import PartitionSpec as P

SWEEPS = 4
STEP = 0.2
NC, NP, NFP = 6, 35, 15
RP = 40
KP = 48
FP = 16
CHUNK = 512
SUB = 128
f32, bf16 = jnp.float32, jnp.bfloat16


def face_nodes():
    lattice = [(r, s, t) for r in range(5) for s in range(5 - r) for t in range(5 - r - s)]
    tests = [
        lambda p: p[2] == 0,
        lambda p: p[1] == 0,
        lambda p: p[0] == 0,
        lambda p: sum(p) == 4,
    ]
    return [[i for i, p in enumerate(lattice) if test(p)] for test in tests]


def constants():
    trace = np.zeros((4 * FP, NP), np.float32)
    for f, nodes in enumerate(face_nodes()):
        for n, node in enumerate(nodes):
            trace[f * FP + n, node] = 1
    trace3 = np.zeros((4 * FP, 3 * KP), np.float32)
    trace3[:, :NP] = trace
    trace3[:, 2 * KP : 2 * KP + NP] = trace
    spread = np.zeros((2, NP, 3 * KP), np.float32)
    for i in range(NP):
        spread[0, i, i] = spread[0, i, 2 * KP + i] = spread[1, i, KP + i] = 1
    lift_spread = np.zeros((2, 4 * NFP, 3 * 4 * FP), np.float32)
    for f in range(4):
        for n in range(NFP):
            row, col = f * NFP + n, f * FP + n
            lift_spread[0, row, col] = lift_spread[0, row, 8 * FP + col] = 1
            lift_spread[1, row, 4 * FP + col] = 1
    trace6 = np.kron(np.eye(NC, dtype=np.float32), trace)
    rows6 = np.kron(np.eye(NC, dtype=np.float32), np.eye(RP, NP, dtype=np.float32))
    cols6 = np.concatenate([rows6.T, rows6.T], axis=1)
    return [jnp.asarray(a, bf16) for a in (trace3, spread, lift_spread, trace6, rows6, cols6)]


def split(x):
    hi = x.astype(bf16)
    return hi, (x - hi.astype(f32)).astype(bf16)


def dot(a, b):
    return jnp.dot(a, b, preferred_element_type=f32)


def kernel(
    el, fields, metric, scale, angles, nb, send_dom, send_part, kind, deriv, lift, binv,
    trace3, spread, lift_spread, trace6, rows6, cols6,
    out,
    fpad, d3, l3, wt, wf, grads, tr, own, recv_n, coef, sel, sel_send, pool, remote, ext, rhs,
    sendbuf, recvbuf, send_sem, recv_sem,
):
    grp, dom = lax.axis_index("group"), lax.axis_index("dom")
    count = lax.axis_size("dom")
    half = count // 2
    fine = jnp.logical_and(grp == 1, dom >= half)
    halves = el // CHUNK
    chunks = 4 * halves
    has_prev, has_next = dom > 0, dom < count - 1
    fine_prev = jnp.logical_and(fine, dom > half)
    fine_next = jnp.logical_and(fine, has_next)

    barrier = pltpu.get_barrier_semaphore()

    @pl.when(has_prev)
    def _():
        pl.semaphore_signal(barrier, inc=1, device_id={"dom": dom - 1})

    @pl.when(has_next)
    def _():
        pl.semaphore_signal(barrier, inc=1, device_id={"dom": dom + 1})

    pl.semaphore_signal(barrier, inc=1, device_id={"group": 1 - grp})

    def slot(f):
        row = nb[f : f + 1, :]
        lane = lax.broadcasted_iota(jnp.int32, (1, el), 1)
        return jnp.where(row < 0, lane + f * el, row)

    def send_list():
        return jnp.concatenate([send_dom[0:1, :], send_dom[1:2, :], send_part[...]], axis=1)

    def pair_copies(step):
        targets = ({"dom": dom - 1}, {"dom": dom + 1}, {"group": 1 - grp})
        lands = (1, 0, 2)
        return [
            pltpu.make_async_remote_copy(
                src_ref=sendbuf.at[step, i],
                dst_ref=recvbuf.at[step, lands[i]],
                send_sem=send_sem.at[step, i],
                recv_sem=recv_sem.at[step, lands[i]],
                device_id=targets[i],
            )
            for i in range(3)
        ]

    def start(step, to_prev, to_next, partner):
        copies = pair_copies(step)

        @pl.when(to_prev)
        def _():
            copies[0].start()

        @pl.when(to_next)
        def _():
            copies[1].start()

        if partner:
            copies[2].start()

    def finish(step, from_prev, from_next, partner):
        copies = pair_copies(step)

        @pl.when(from_prev)
        def _():
            copies[0].wait_send()
            copies[1].wait_recv()
            remote[0] = recvbuf[step, 0]

        @pl.when(from_next)
        def _():
            copies[1].wait_send()
            copies[0].wait_recv()
            remote[1] = recvbuf[step, 1]

        if partner:
            copies[2].wait()
            remote[2] = recvbuf[step, 2]

    def pool_store(f, x):
        rows = x.shape[0]
        hi = x.astype(bf16).astype(f32)
        both = jnp.concatenate([hi, x - hi], axis=0).astype(bf16)
        for k in range(halves):
            h = f * halves + k
            pool[h * 2 * rows : (h + 1) * 2 * rows, :] = both[:, k * CHUNK : (k + 1) * CHUNK]

    def pick(y, which, rows):
        total = jnp.zeros((rows, y.shape[1]), f32)
        for h in range(chunks):
            at = h * 2 * rows
            value = y[at : at + rows] + y[at + rows : at + 2 * rows]
            total = jnp.where(which == h, value, total)
        return total

    def outgoing(step, rows):
        y = dot(pool[: chunks * 2 * rows, :], sel_send[...])
        picked = pick(y, send_list() // CHUNK, rows)
        for i in range(3):
            sendbuf[step, i, 0:rows, :] = picked[:, i * SUB : (i + 1) * SUB]

    def gather_local(rows, dest):
        for f in range(4):
            y = dot(pool[: chunks * 2 * rows, :], sel[:, f * el : (f + 1) * el])
            dest[f] = pick(y, slot(f) // CHUNK, rows)

    def gather_remote(rows, dest):
        x = jnp.concatenate([remote[i, 0:rows, :] for i in range(3)], axis=1)
        hi = x.astype(bf16).astype(f32)
        both = jnp.concatenate([hi, x - hi], axis=0).astype(bf16)
        for f in range(4):
            y = dot(both, sel[0 : 3 * SUB, f * el : (f + 1) * el])
            dest[f] = jnp.where(slot(f) // CHUNK == chunks, y[:rows] + y[rows:], dest[f])

    polar, azimuth = angles[0], angles[1]
    parts = (jnp.sin(polar), jnp.cos(polar), jnp.sin(azimuth), jnp.cos(azimuth))
    own[...] = jnp.zeros_like(own)
    for f in range(4):
        for i in range(4):
            own[f, i : i + 1, :] = parts[i][f : f + 1, :]
        w = 0.5 * scale[f : f + 1, :]
        sa, ca, sb, cb = (p[f : f + 1, :] for p in parts)
        for i, row in enumerate((w * ca * cb, w * ca * sb, -w * sa, -w * sb, w * cb)):
            coef[f, i : i + 1, :] = row
        pool_store(f, own[f])
        down = lax.broadcasted_iota(jnp.int32, (CHUNK, el), 0)
        sel[:, f * el : (f + 1) * el] = jnp.where(down == slot(f) % CHUNK, 1.0, 0.0).astype(bf16)
    down = lax.broadcasted_iota(jnp.int32, (CHUNK, 3 * SUB), 0)
    sel_send[...] = jnp.where(down == send_list() % CHUNK, 1.0, 0.0).astype(bf16)
    remote[...] = jnp.zeros_like(remote)
    sendbuf[0] = jnp.zeros_like(sendbuf[0])

    outgoing(0, 8)
    pl.semaphore_wait(
        barrier, 1 + has_prev.astype(jnp.int32) + has_next.astype(jnp.int32)
    )
    start(0, has_prev, has_next, True)

    gather_local(8, recv_n)

    fpad[...] = jnp.zeros_like(fpad)
    d3[...] = jnp.zeros_like(d3)
    l3[...] = jnp.zeros_like(l3)
    for b in range(3):
        hi, lo = split(deriv[b])
        d3[b * RP : b * RP + NP, :] = dot(hi, spread[0]) + dot(lo, spread[1])
    d3[3 * RP : 3 * RP + 4 * FP, :] = trace3[...].astype(f32)
    hi, lo = split(lift[...])
    l3[0:NP, :] = dot(hi, lift_spread[0]) + dot(lo, lift_spread[1])
    d3b = d3[...].astype(bf16)
    for c in range(NC):
        fpad[c, 0:NP, :] = fields[c]
        hi, lo = split(fpad[c])
        y = dot(d3b, jnp.concatenate([hi, hi, lo], axis=0))
        grads[c] = y[: 3 * RP]
        tr[c * 4 * FP : (c + 1) * 4 * FP, :] = y[3 * RP :]

    def trace_pq(f, n_ref, sign):
        at = [tr[c * 4 * FP + f * FP : c * 4 * FP + (f + 1) * FP, :] for c in range(NC)]
        sa, ca, sb, cb = (n_ref[f, i : i + 1, :] for i in range(4))
        if sign is not None:
            at[:3] = [sign * e for e in at[:3]]
        e_t = ca * (cb * at[0] + sb * at[1]) - sa * at[2]
        e_p = cb * at[1] - sb * at[0]
        h_t = ca * (cb * at[3] + sb * at[4]) - sa * at[5]
        h_p = cb * at[4] - sb * at[3]
        return jnp.concatenate([h_p - e_t, -h_t - e_p], axis=0)

    def fill_pool():
        for f in range(4):
            sign = jnp.where(nb[f : f + 1, :] < 0, -1.0, 1.0)
            pool_store(f, trace_pq(f, recv_n, sign))

    def lifted(pq):
        for c in range(NC):
            rows = []
            for f in range(4):
                p, q = pq[f][:FP], pq[f][FP:]
                a, b = (p, q) if c < 3 else (q, -p)
                k = c % 3
                row = coef[f, k : k + 1, :] * a
                if k < 2:
                    row = row + coef[f, 3 + k : 4 + k, :] * b
                rows.append(row)
            hi, lo = split(jnp.concatenate(rows, axis=0))
            yield c, dot(l3[...].astype(bf16), jnp.concatenate([hi, hi, lo], axis=0))

    finish(0, has_prev, has_next, True)
    gather_remote(8, recv_n)
    fill_pool()
    outgoing(1, 2 * FP)
    start(1, has_prev, has_next, True)
    gather_local(2 * FP, ext)

    @pl.when(fine)
    def _():
        for k in range(binv.shape[0]):
            b2 = dot(binv[k], cols6[...]).astype(bf16)
            wt[k] = dot(trace6[...], b2).astype(bf16)
            wf[k] = dot(rows6[...], b2).astype(bf16)

    remote[...] = jnp.zeros_like(remote)
    finish(1, has_prev, has_next, True)
    gather_remote(2 * FP, ext)

    @pl.when(jnp.logical_not(fine))
    def _():
        pq = [trace_pq(f, own, None) - ext[f] for f in range(4)]

        def along(c, axis):
            return sum(
                metric[3 * axis + b : 3 * axis + b + 1, :] * grads[c, b * RP : (b + 1) * RP, :]
                for b in range(3)
            )

        for c, s in lifted(pq):
            k, other = c % 3, 3 - 3 * (c // 3)
            one, two = (k + 1) % 3, (k + 2) % 3
            curl = along(other + two, one) - along(other + one, two)
            vol = curl if c < 3 else -curl
            out[c] = (fpad[c, 0:RP, :] + STEP * (vol + s))[:NP]

    @pl.when(fine)
    def _():
        def right_side():
            terms = [
                fpad[c, 0:RP, :] - STEP * s for c, s in lifted([ext[f] for f in range(4)])
            ]
            hi, lo = split(jnp.concatenate(terms, axis=0))
            rhs[0 : NC * RP, :] = hi
            rhs[NC * RP : 2 * NC * RP, :] = lo

        def blocks(weights, k):
            mask = jnp.where(kind[...] == k + 1, 1.0, 0.0).astype(bf16)
            return dot(weights[k], rhs[...] * mask)

        def sweep(no, carry):
            right_side()
            tr[...] = blocks(wt, 0)
            for k in range(1, binv.shape[0]):
                tr[...] += blocks(wt, k)
            fill_pool()
            outgoing(no, 2 * FP)
            start(no, fine_prev, fine_next, False)
            gather_local(2 * FP, ext)
            finish(no, fine_prev, fine_next, False)
            gather_remote(2 * FP, ext)
            return carry

        lax.fori_loop(2, SWEEPS + 1, sweep, 0)
        right_side()
        total = blocks(wf, 0)
        for k in range(1, binv.shape[0]):
            total += blocks(wf, k)
        for c in range(NC):
            out[c] = total[c * RP : c * RP + NP]


def shards(*args):
    (fields, metric, scale, angles, nb, send_dom, send_part, kind, deriv, lift, binv) = args
    el = fields.shape[2]
    kinds = binv.shape[0]
    operands = [
        fields, metric, scale, angles, nb, send_dom, send_part.reshape(1, -1),
        kind.reshape(1, -1), deriv, lift, binv, *constants(),
    ]
    vmem = pltpu.VMEM
    return pl.pallas_call(
        functools.partial(kernel, el),
        out_shape=jax.ShapeDtypeStruct(fields.shape, f32),
        in_specs=[pl.BlockSpec(memory_space=vmem)] * len(operands),
        out_specs=pl.BlockSpec(memory_space=vmem),
        scratch_shapes=[
            vmem((NC, KP, el), f32),
            vmem((3 * RP + 4 * FP, 3 * KP), f32),
            vmem((RP, 12 * FP), f32),
            vmem((kinds, NC * 4 * FP, 2 * NC * RP), bf16),
            vmem((kinds, NC * RP, 2 * NC * RP), bf16),
            vmem((NC, 3 * RP, el), f32),
            vmem((NC * 4 * FP, el), f32),
            vmem((4, 8, el), f32),
            vmem((4, 8, el), f32),
            vmem((4, 8, el), f32),
            vmem((CHUNK, 4 * el), bf16),
            vmem((CHUNK, 3 * SUB), bf16),
            vmem((4 * (el // CHUNK) * 4 * FP, CHUNK), bf16),
            vmem((3, 2 * FP, SUB), f32),
            vmem((4, 2 * FP, el), f32),
            vmem((2 * NC * RP, el), bf16),
            vmem((SWEEPS + 1, 3, 2 * FP, SUB), f32),
            vmem((SWEEPS + 1, 3, 2 * FP, SUB), f32),
            pltpu.SemaphoreType.DMA((SWEEPS + 1, 3)),
            pltpu.SemaphoreType.DMA((SWEEPS + 1, 3)),
        ],
        compiler_params=pltpu.CompilerParams(
            collective_id=0, has_side_effects=True, vmem_limit_bytes=56 * 2**20
        ),
    )(*operands)


def solution(mesh):
    both = ("group", "dom")
    in_specs = (
        P(None, None, both), P(None, both), P(None, both), P(None, None, both), P(None, both),
        P(None, both), P(both), P(both), P(), P(), P(),
    )
    return jax.shard_map(
        shards, mesh=mesh, in_specs=in_specs, out_specs=P(None, None, both), check_vma=False
    )
```

profile of v0, /device:TPU:23, one launch (start us, length us, event | category | flops | bytes accessed | tf_op | source)
XLA Modules:
  0.0 40.0 jit_solution(5542499621787955068)
XLA Ops:
  0.0 37.7 %shard_map.163 = f32[6,35,1024]{2,1,0:T(8,128)} custom-call(f32[6,35,1024]{2,1,0:T(8,128)} %fields.1, f32[9,1024]{1,0:T(8,128)} %metric.1, f32[4,1024]{1,0:T(4,128)} %scale.1, f32[2,4,1024]{2,1,0:T(4,128)} %angles.1, s32[4,1024]{1,0:T(4,128)} %nb.1, s32[2,128]{1,0:T(2,128)} %send_dom.1, s32[1,128]{1,0:T(1,128)} %bitcast.3, s32[1,1024]{1,0:T(1,128)} %bitcast.2, ...), custom_call_target="tpu_custom_call" | custom-call | tf_op jit(solution)/shard_map/pallas_call | solution.py:337
  37.7 2.2 %copy.19 = f32[6,35,1024]{2,1,0:T(8,128)} copy(f32[6,35,1024]{2,1,0:T(8,128)} %shard_map.163) | data formatting | bytes 1720320
where the time goes:
time: 40.1 us; the launch traced here: 40 us
  Pallas kernels  37.7 us (94%)
  local copies, waits for them, and re-layouts  2.25 us (6%)
    pallas_call x1, Pallas kernels, shards(): pl.pallas_call(functools.partial(kernel, el), out_shape=jax.ShapeDtypeStr...  37.7 us
    unnamed x1, local copies, waits for them, and re-layouts  2.25 us

commit v1 on v0

--- a/solution.py
+++ b/solution.py
@@ -14,6 +14,7 @@
 RP = 40
 KP = 48
 FP = 16
+BK = 512
 CHUNK = 512
 SUB = 128
 f32, bf16 = jnp.float32, jnp.bfloat16
@@ -49,7 +50,8 @@
             lift_spread[1, row, 4 * FP + col] = 1
     trace6 = np.kron(np.eye(NC, dtype=np.float32), trace)
     rows6 = np.kron(np.eye(NC, dtype=np.float32), np.eye(RP, NP, dtype=np.float32))
-    cols6 = np.concatenate([rows6.T, rows6.T], axis=1)
+    cols6 = np.zeros((NC * NP, BK), np.float32)
+    cols6[:, : 2 * NC * RP] = np.concatenate([rows6.T, rows6.T], axis=1)
     return [jnp.asarray(a, bf16) for a in (trace3, spread, lift_spread, trace6, rows6, cols6)]
 
 
@@ -66,8 +68,8 @@
     el, fields, metric, scale, angles, nb, send_dom, send_part, kind, deriv, lift, binv,
     trace3, spread, lift_spread, trace6, rows6, cols6,
     out,
-    fpad, d3, l3, wt, wf, grads, tr, own, recv_n, coef, sel, sel_send, pool, remote, ext, rhs,
-    sendbuf, recvbuf, send_sem, recv_sem,
+    fpad, d3, l3, wt, wf, grads, tr, own, recv_n, coef, sel, sel_send, pool, remote, ext,
+    base, lb, rhs6, sendbuf, recvbuf, send_sem, recv_sem,
 ):
     grp, dom = lax.axis_index("group"), lax.axis_index("dom")
     count = lax.axis_size("dom")
@@ -154,32 +156,46 @@
             h = f * halves + k
             pool[h * 2 * rows : (h + 1) * 2 * rows, :] = both[:, k * CHUNK : (k + 1) * CHUNK]
 
-    def pick(y, which, rows):
-        total = jnp.zeros((rows, y.shape[1]), f32)
-        for h in range(chunks):
+    def pick(y, which, rows, count, total=None):
+        if total is None:
+            total = jnp.zeros((rows, y.shape[1]), f32)
+        for h in range(count):
             at = h * 2 * rows
             value = y[at : at + rows] + y[at + rows : at + 2 * rows]
             total = jnp.where(which == h, value, total)
         return total
 
-    def outgoing(step, rows):
-        y = dot(pool[: chunks * 2 * rows, :], sel_send[...])
-        picked = pick(y, send_list() // CHUNK, rows)
-        for i in range(3):
+    def outgoing(step, rows, lists):
+        cols = lists * SUB
+        y = dot(pool[: chunks * 2 * rows, :], sel_send[:, :cols])
+        picked = pick(y, (send_list() // CHUNK)[:, :cols], rows, chunks)
+        for i in range(lists):
             sendbuf[step, i, 0:rows, :] = picked[:, i * SUB : (i + 1) * SUB]
 
+    def arrived(rows, lists):
+        x = jnp.concatenate([remote[i, 0:rows, :] for i in range(lists)], axis=1)
+        hi = x.astype(bf16).astype(f32)
+        return jnp.concatenate([hi, x - hi], axis=0).astype(bf16)
+
+    def gather_all(rows, dest):
+        at = chunks * 2 * rows
+        pool[at : at + 2 * rows, :] = jnp.zeros((2 * rows, CHUNK), bf16)
+        pool[at : at + 2 * rows, 0 : 3 * SUB] = arrived(rows, 3)
+        for f in range(4):
+            y = dot(pool[: at + 2 * rows, :], sel[:, f * el : (f + 1) * el])
+            dest[f] = pick(y, slot(f) // CHUNK, rows, chunks + 1)
+
     def gather_local(rows, dest):
         for f in range(4):
             y = dot(pool[: chunks * 2 * rows, :], sel[:, f * el : (f + 1) * el])
-            dest[f] = pick(y, slot(f) // CHUNK, rows)
-
-    def gather_remote(rows, dest):
-        x = jnp.concatenate([remote[i, 0:rows, :] for i in range(3)], axis=1)
-        hi = x.astype(bf16).astype(f32)
-        both = jnp.concatenate([hi, x - hi], axis=0).astype(bf16)
-        for f in range(4):
-            y = dot(both, sel[0 : 3 * SUB, f * el : (f + 1) * el])
-            dest[f] = jnp.where(slot(f) // CHUNK == chunks, y[:rows] + y[rows:], dest[f])
+            dest[f] = pick(y, slot(f) // CHUNK, rows, chunks, base[f])
+
+    def gather_dom(rows, dest):
+        both = arrived(rows, 2)
+        for f in range(4):
+            y = dot(both, sel[0 : 2 * SUB, f * el : (f + 1) * el])
+            there = slot(f) // (2 * SUB) == 4 * el // (2 * SUB)
+            dest[f] = jnp.where(there, y[:rows] + y[rows:], dest[f])
 
     polar, azimuth = angles[0], angles[1]
     parts = (jnp.sin(polar), jnp.cos(polar), jnp.sin(azimuth), jnp.cos(azimuth))
@@ -192,20 +208,20 @@
         for i, row in enumerate((w * ca * cb, w * ca * sb, -w * sa, -w * sb, w * cb)):
             coef[f, i : i + 1, :] = row
         pool_store(f, own[f])
-        down = lax.broadcasted_iota(jnp.int32, (CHUNK, el), 0)
-        sel[:, f * el : (f + 1) * el] = jnp.where(down == slot(f) % CHUNK, 1.0, 0.0).astype(bf16)
     down = lax.broadcasted_iota(jnp.int32, (CHUNK, 3 * SUB), 0)
     sel_send[...] = jnp.where(down == send_list() % CHUNK, 1.0, 0.0).astype(bf16)
     remote[...] = jnp.zeros_like(remote)
     sendbuf[0] = jnp.zeros_like(sendbuf[0])
 
-    outgoing(0, 8)
+    outgoing(0, 8, 3)
     pl.semaphore_wait(
         barrier, 1 + has_prev.astype(jnp.int32) + has_next.astype(jnp.int32)
     )
     start(0, has_prev, has_next, True)
 
-    gather_local(8, recv_n)
+    for f in range(4):
+        down = lax.broadcasted_iota(jnp.int32, (CHUNK, el), 0)
+        sel[:, f * el : (f + 1) * el] = jnp.where(down == slot(f) % CHUNK, 1.0, 0.0).astype(bf16)
 
     fpad[...] = jnp.zeros_like(fpad)
     d3[...] = jnp.zeros_like(d3)
@@ -216,6 +232,10 @@
     d3[3 * RP : 3 * RP + 4 * FP, :] = trace3[...].astype(f32)
     hi, lo = split(lift[...])
     l3[0:NP, :] = dot(hi, lift_spread[0]) + dot(lo, lift_spread[1])
+    lane = lax.broadcasted_iota(jnp.int32, l3.shape, 1)
+    lb[...] = jnp.concatenate(
+        [jnp.where(lane // FP % 4 == f, l3[...], 0.0) for f in range(4)], axis=0
+    ).astype(bf16)
     d3b = d3[...].astype(bf16)
     for c in range(NC):
         fpad[c, 0:NP, :] = fields[c]
@@ -241,36 +261,39 @@
             pool_store(f, trace_pq(f, recv_n, sign))
 
     def lifted(pq):
+        halves_of = []
+        for at in (0, FP):
+            hi, lo = split(jnp.concatenate([pq[f][at : at + FP] for f in range(4)], axis=0))
+            halves_of.append(dot(lb[...], jnp.concatenate([hi, hi, lo], axis=0)))
+        lp, lq = halves_of
         for c in range(NC):
-            rows = []
+            k, total = c % 3, 0.0
+            a, b = (lp, lq) if c < 3 else (lq, lp)
             for f in range(4):
-                p, q = pq[f][:FP], pq[f][FP:]
-                a, b = (p, q) if c < 3 else (q, -p)
-                k = c % 3
-                row = coef[f, k : k + 1, :] * a
+                at = slice(f * RP, (f + 1) * RP)
+                total = total + coef[f, k : k + 1, :] * a[at]
                 if k < 2:
-                    row = row + coef[f, 3 + k : 4 + k, :] * b
-                rows.append(row)
-            hi, lo = split(jnp.concatenate(rows, axis=0))
-            yield c, dot(l3[...].astype(bf16), jnp.concatenate([hi, hi, lo], axis=0))
+                    term = coef[f, 3 + k : 4 + k, :] * b[at]
+                    total = total + term if c < 3 else total - term
+            yield c, total
 
     finish(0, has_prev, has_next, True)
-    gather_remote(8, recv_n)
+    gather_all(8, recv_n)
     fill_pool()
-    outgoing(1, 2 * FP)
+    outgoing(1, 2 * FP, 3)
     start(1, has_prev, has_next, True)
-    gather_local(2 * FP, ext)
 
     @pl.when(fine)
     def _():
+        rhs6[...] = jnp.zeros_like(rhs6)
         for k in range(binv.shape[0]):
             b2 = dot(binv[k], cols6[...]).astype(bf16)
-            wt[k] = dot(trace6[...], b2).astype(bf16)
-            wf[k] = dot(rows6[...], b2).astype(bf16)
+            wt[:, k * BK : (k + 1) * BK] = dot(trace6[...], b2).astype(bf16)
+            wf[:, k * BK : (k + 1) * BK] = dot(rows6[...], b2).astype(bf16)
 
     remote[...] = jnp.zeros_like(remote)
     finish(1, has_prev, has_next, True)
-    gather_remote(2 * FP, ext)
+    gather_all(2 * FP, ext)
 
     @pl.when(jnp.logical_not(fine))
     def _():
@@ -295,32 +318,28 @@
             terms = [
                 fpad[c, 0:RP, :] - STEP * s for c, s in lifted([ext[f] for f in range(4)])
             ]
-            hi, lo = split(jnp.concatenate(terms, axis=0))
-            rhs[0 : NC * RP, :] = hi
-            rhs[NC * RP : 2 * NC * RP, :] = lo
-
-        def blocks(weights, k):
-            mask = jnp.where(kind[...] == k + 1, 1.0, 0.0).astype(bf16)
-            return dot(weights[k], rhs[...] * mask)
+            both = jnp.concatenate(split(jnp.concatenate(terms, axis=0)), axis=0)
+            for k in range(binv.shape[0]):
+                mask = jnp.where(kind[...] == k + 1, 1.0, 0.0).astype(bf16)
+                rhs6[k * BK : k * BK + 2 * NC * RP, :] = both * mask
+
+        for f in range(4):
+            base[f] = jnp.where(slot(f) >= 4 * el + 2 * SUB, ext[f], 0.0)
 
         def sweep(no, carry):
             right_side()
-            tr[...] = blocks(wt, 0)
-            for k in range(1, binv.shape[0]):
-                tr[...] += blocks(wt, k)
+            tr[...] = dot(wt[...], rhs6[...])
             fill_pool()
-            outgoing(no, 2 * FP)
+            outgoing(no, 2 * FP, 2)
             start(no, fine_prev, fine_next, False)
             gather_local(2 * FP, ext)
             finish(no, fine_prev, fine_next, False)
-            gather_remote(2 * FP, ext)
+            gather_dom(2 * FP, ext)
             return carry
 
         lax.fori_loop(2, SWEEPS + 1, sweep, 0)
         right_side()
-        total = blocks(wf, 0)
-        for k in range(1, binv.shape[0]):
-            total += blocks(wf, k)
+        total = dot(wf[...], rhs6[...])
         for c in range(NC):
             out[c] = total[c * RP : c * RP + NP]
 
@@ -343,8 +362,8 @@
             vmem((NC, KP, el), f32),
             vmem((3 * RP + 4 * FP, 3 * KP), f32),
             vmem((RP, 12 * FP), f32),
-            vmem((kinds, NC * 4 * FP, 2 * NC * RP), bf16),
-            vmem((kinds, NC * RP, 2 * NC * RP), bf16),
+            vmem((NC * 4 * FP, kinds * BK), bf16),
+            vmem((NC * RP, kinds * BK), bf16),
             vmem((NC, 3 * RP, el), f32),
             vmem((NC * 4 * FP, el), f32),
             vmem((4, 8, el), f32),
@@ -352,10 +371,12 @@
             vmem((4, 8, el), f32),
             vmem((CHUNK, 4 * el), bf16),
             vmem((CHUNK, 3 * SUB), bf16),
-            vmem((4 * (el // CHUNK) * 4 * FP, CHUNK), bf16),
+            vmem(((4 * (el // CHUNK) + 1) * 4 * FP, CHUNK), bf16),
             vmem((3, 2 * FP, SUB), f32),
             vmem((4, 2 * FP, el), f32),
-            vmem((2 * NC * RP, el), bf16),
+            vmem((4, 2 * FP, el), f32),
+            vmem((4 * RP, 12 * FP), bf16),
+            vmem((kinds * BK, el), bf16),
             vmem((SWEEPS + 1, 3, 2 * FP, SUB), f32),
             vmem((SWEEPS + 1, 3, 2 * FP, SUB), f32),
             pltpu.SemaphoreType.DMA((SWEEPS + 1, 3)),

time: 40.1 us -> 41.5 us (1.035)
  Pallas kernels: 37.7 us -> 39.1 us
    pallas_call x1, Pallas kernels: 37.7 us -> 39.1 us  [shards(): pl.pallas_call(functools.partial(kernel, el), out_shape=jax.ShapeDtypeStr...]
where the time goes in v1:
time: 41.5 us; the launch traced here: 41.3 us
  Pallas kernels  39.1 us (94%)
  local copies, waits for them, and re-layouts  2.25 us (5%)
    pallas_call x1, Pallas kernels, shards(): pl.pallas_call(functools.partial(kernel, el), out_shape=jax.ShapeDtypeStr...  39.1 us
    unnamed x1, local copies, waits for them, and re-layouts  2.25 us

profile of v1, /device:TPU:23, one launch (start us, length us, event | category | flops | bytes accessed | tf_op | source)
XLA Modules:
  0.0 41.3 jit_solution(17862499428304654751)
XLA Ops:
  0.0 39.1 %shard_map.163 = f32[6,35,1024]{2,1,0:T(8,128)} custom-call(f32[6,35,1024]{2,1,0:T(8,128)} %fields.1, f32[9,1024]{1,0:T(8,128)} %metric.1, f32[4,1024]{1,0:T(4,128)} %scale.1, f32[2,4,1024]{2,1,0:T(4,128)} %angles.1, s32[4,1024]{1,0:T(4,128)} %nb.1, s32[2,128]{1,0:T(2,128)} %send_dom.1, s32[1,128]{1,0:T(1,128)} %bitcast.3, s32[1,1024]{1,0:T(1,128)} %bitcast.2, ...), custom_call_target="tpu_custom_call" | custom-call | tf_op jit(solution)/shard_map/pallas_call | solution.py:356
  39.1 2.2 %copy.19 = f32[6,35,1024]{2,1,0:T(8,128)} copy(f32[6,35,1024]{2,1,0:T(8,128)} %shard_map.163) | data formatting | bytes 1720320

commit v2 on v1

--- a/solution.py
+++ b/solution.py
@@ -50,8 +50,8 @@
             lift_spread[1, row, 4 * FP + col] = 1
     trace6 = np.kron(np.eye(NC, dtype=np.float32), trace)
     rows6 = np.kron(np.eye(NC, dtype=np.float32), np.eye(RP, NP, dtype=np.float32))
-    cols6 = np.zeros((NC * NP, BK), np.float32)
-    cols6[:, : 2 * NC * RP] = np.concatenate([rows6.T, rows6.T], axis=1)
+    cols6 = np.zeros((NC * NP, BK // 2), np.float32)
+    cols6[:, : NC * RP] = rows6.T
     return [jnp.asarray(a, bf16) for a in (trace3, spread, lift_spread, trace6, rows6, cols6)]
 
 
@@ -185,16 +185,19 @@
             y = dot(pool[: at + 2 * rows, :], sel[:, f * el : (f + 1) * el])
             dest[f] = pick(y, slot(f) // CHUNK, rows, chunks + 1)
 
-    def gather_local(rows, dest):
+    def gather_local(rows, dest, start_from=None):
         for f in range(4):
             y = dot(pool[: chunks * 2 * rows, :], sel[:, f * el : (f + 1) * el])
-            dest[f] = pick(y, slot(f) // CHUNK, rows, chunks, base[f])
-
-    def gather_dom(rows, dest):
-        both = arrived(rows, 2)
+            dest[f] = pick(
+                y, slot(f) // CHUNK, rows, chunks, None if start_from is None else start_from[f]
+            )
+
+    def gather_late(rows, dest, lists):
+        both = arrived(rows, lists)
         for f in range(4):
-            y = dot(both, sel[0 : 2 * SUB, f * el : (f + 1) * el])
-            there = slot(f) // (2 * SUB) == 4 * el // (2 * SUB)
+            y = dot(both, sel[0 : lists * SUB, f * el : (f + 1) * el])
+            here = slot(f)
+            there = jnp.logical_and(here >= 4 * el, here < 4 * el + lists * SUB)
             dest[f] = jnp.where(there, y[:rows] + y[rows:], dest[f])
 
     polar, azimuth = angles[0], angles[1]
@@ -277,23 +280,26 @@
                     total = total + term if c < 3 else total - term
             yield c, total
 
+    @pl.when(fine)
+    def _():
+        rhs6[...] = jnp.zeros_like(rhs6)
+        for k in range(binv.shape[0]):
+            b2 = dot(binv[k], cols6[...]).astype(bf16)
+            for weights, select in ((wt, trace6), (wf, rows6)):
+                half_block = dot(select[...], b2).astype(bf16)
+                for at in (k * BK, k * BK + BK // 2):
+                    weights[:, at : at + BK // 2] = half_block
+
     finish(0, has_prev, has_next, True)
     gather_all(8, recv_n)
     fill_pool()
     outgoing(1, 2 * FP, 3)
     start(1, has_prev, has_next, True)
 
-    @pl.when(fine)
-    def _():
-        rhs6[...] = jnp.zeros_like(rhs6)
-        for k in range(binv.shape[0]):
-            b2 = dot(binv[k], cols6[...]).astype(bf16)
-            wt[:, k * BK : (k + 1) * BK] = dot(trace6[...], b2).astype(bf16)
-            wf[:, k * BK : (k + 1) * BK] = dot(rows6[...], b2).astype(bf16)
-
+    gather_local(2 * FP, ext)
     remote[...] = jnp.zeros_like(remote)
     finish(1, has_prev, has_next, True)
-    gather_all(2 * FP, ext)
+    gather_late(2 * FP, ext, 3)
 
     @pl.when(jnp.logical_not(fine))
     def _():
@@ -318,10 +324,11 @@
             terms = [
                 fpad[c, 0:RP, :] - STEP * s for c, s in lifted([ext[f] for f in range(4)])
             ]
-            both = jnp.concatenate(split(jnp.concatenate(terms, axis=0)), axis=0)
+            hi, lo = split(jnp.concatenate(terms, axis=0))
             for k in range(binv.shape[0]):
                 mask = jnp.where(kind[...] == k + 1, 1.0, 0.0).astype(bf16)
-                rhs6[k * BK : k * BK + 2 * NC * RP, :] = both * mask
+                for at, part in ((k * BK, hi), (k * BK + BK // 2, lo)):
+                    rhs6[at : at + NC * RP, :] = part * mask
 
         for f in range(4):
             base[f] = jnp.where(slot(f) >= 4 * el + 2 * SUB, ext[f], 0.0)
@@ -332,9 +339,9 @@
             fill_pool()
             outgoing(no, 2 * FP, 2)
             start(no, fine_prev, fine_next, False)
-            gather_local(2 * FP, ext)
+            gather_local(2 * FP, ext, base)
             finish(no, fine_prev, fine_next, False)
-            gather_dom(2 * FP, ext)
+            gather_late(2 * FP, ext, 2)
             return carry
 
         lax.fori_loop(2, SWEEPS + 1, sweep, 0)
@@ -342,6 +349,24 @@
         total = dot(wf[...], rhs6[...])
         for c in range(NC):
             out[c] = total[c * RP : c * RP + NP]
+
+
+def move_kernel(source, target, sems):
+    copies = [pltpu.make_async_copy(source.at[c], target.at[c], sems.at[c]) for c in range(NC)]
+    for copy in copies:
+        copy.start()
+    for copy in copies:
+        copy.wait()
+
+
+def moved(x):
+    return pl.pallas_call(
+        move_kernel,
+        out_shape=jax.ShapeDtypeStruct(x.shape, x.dtype),
+        in_specs=[pl.BlockSpec(memory_space=pl.ANY)],
+        out_specs=pl.BlockSpec(memory_space=pl.ANY),
+        scratch_shapes=[pltpu.SemaphoreType.DMA((NC,))],
+    )(x)
 
 
 def shards(*args):
@@ -353,7 +378,7 @@
         kind.reshape(1, -1), deriv, lift, binv, *constants(),
     ]
     vmem = pltpu.VMEM
-    return pl.pallas_call(
+    result = pl.pallas_call(
         functools.partial(kernel, el),
         out_shape=jax.ShapeDtypeStruct(fields.shape, f32),
         in_specs=[pl.BlockSpec(memory_space=vmem)] * len(operands),
@@ -386,6 +411,7 @@
             collective_id=0, has_side_effects=True, vmem_limit_bytes=56 * 2**20
         ),
     )(*operands)
+    return moved(result)
 
 
 def solution(mesh):

time: 41.5 us -> 69.7 us (1.68)
  Pallas kernels: 39.1 us -> 69.4 us
  local copies, waits for them, and re-layouts: 2.25 us -> 0 us
    pallas_call x0 -> x1, Pallas kernels: none -> 30.9 us  [moved(): pl.pallas_call(move_kernel, out_shape=jax.ShapeDtypeStruct(x.shape, x.dty...]
    unnamed x1 -> x0, local copies, waits for them, and re-layouts: 2.25 us -> none
where the time goes in v2:
time: 69.7 us; the launch traced here: 69.6 us
  Pallas kernels  69.4 us (100%)
    pallas_call x1, Pallas kernels, shards(): pl.pallas_call(functools.partial(kernel, el), out_shape=jax.ShapeDtypeStr...  38.5 us
    pallas_call x1, Pallas kernels, moved(): pl.pallas_call(move_kernel, out_shape=jax.ShapeDtypeStruct(x.shape, x.dty...  30.9 us

profile of v2, /device:TPU:23, one launch (start us, length us, event | category | flops | bytes accessed | tf_op | source)
XLA Modules:
  0.0 69.6 jit_solution(8653088071675034464)
XLA Ops:
  0.0 38.5 %shard_map.163.source = f32[6,35,1024]{2,1,0:T(8,128)} custom-call(f32[6,35,1024]{2,1,0:T(8,128)} %fields.1, f32[9,1024]{1,0:T(8,128)} %metric.1, f32[4,1024]{1,0:T(4,128)} %scale.1, f32[2,4,1024]{2,1,0:T(4,128)} %angles.1, s32[4,1024]{1,0:T(4,128)} %nb.1, s32[2,128]{1,0:T(2,128)} %send_dom.1, s32[1,128]{1,0:T(1,128)} %bitcast.3, s32[1,1024]{1,0:T(1,128)} %bitcast.2, ...), custom_call_target="tpu_custom_call" | custom-call | tf_op jit(solution)/shard_map/pallas_call | solution.py:381
  38.5 30.9 %shard_map.164 = f32[6,35,1024]{2,1,0:T(8,128)} custom-call(f32[6,35,1024]{2,1,0:T(8,128)} %shard_map.163.source), custom_call_target="tpu_custom_call" | custom-call | tf_op jit(solution)/shard_map/pallas_call | solution.py:363

commit v3 on v0

--- a/solution.py
+++ b/solution.py
@@ -67,7 +67,7 @@
     trace3, spread, lift_spread, trace6, rows6, cols6,
     out,
     fpad, d3, l3, wt, wf, grads, tr, own, recv_n, coef, sel, sel_send, pool, remote, ext, rhs,
-    sendbuf, recvbuf, send_sem, recv_sem,
+    base, sendbuf, recvbuf, send_sem, recv_sem,
 ):
     grp, dom = lax.axis_index("group"), lax.axis_index("dom")
     count = lax.axis_size("dom")
@@ -154,32 +154,36 @@
             h = f * halves + k
             pool[h * 2 * rows : (h + 1) * 2 * rows, :] = both[:, k * CHUNK : (k + 1) * CHUNK]
 
-    def pick(y, which, rows):
-        total = jnp.zeros((rows, y.shape[1]), f32)
+    def pick(y, which, rows, total=None):
+        if total is None:
+            total = jnp.zeros((rows, y.shape[1]), f32)
         for h in range(chunks):
             at = h * 2 * rows
             value = y[at : at + rows] + y[at + rows : at + 2 * rows]
             total = jnp.where(which == h, value, total)
         return total
 
-    def outgoing(step, rows):
-        y = dot(pool[: chunks * 2 * rows, :], sel_send[...])
-        picked = pick(y, send_list() // CHUNK, rows)
-        for i in range(3):
+    def outgoing(step, rows, lists=3):
+        y = dot(pool[: chunks * 2 * rows, :], sel_send[:, : lists * SUB])
+        picked = pick(y, (send_list() // CHUNK)[:, : lists * SUB], rows)
+        for i in range(lists):
             sendbuf[step, i, 0:rows, :] = picked[:, i * SUB : (i + 1) * SUB]
 
-    def gather_local(rows, dest):
+    def gather_local(rows, dest, start_from=None):
         for f in range(4):
             y = dot(pool[: chunks * 2 * rows, :], sel[:, f * el : (f + 1) * el])
-            dest[f] = pick(y, slot(f) // CHUNK, rows)
-
-    def gather_remote(rows, dest):
-        x = jnp.concatenate([remote[i, 0:rows, :] for i in range(3)], axis=1)
+            under = None if start_from is None else start_from[f]
+            dest[f] = pick(y, slot(f) // CHUNK, rows, under)
+
+    def gather_remote(rows, dest, lists=3):
+        x = jnp.concatenate([remote[i, 0:rows, :] for i in range(lists)], axis=1)
         hi = x.astype(bf16).astype(f32)
         both = jnp.concatenate([hi, x - hi], axis=0).astype(bf16)
         for f in range(4):
-            y = dot(both, sel[0 : 3 * SUB, f * el : (f + 1) * el])
-            dest[f] = jnp.where(slot(f) // CHUNK == chunks, y[:rows] + y[rows:], dest[f])
+            y = dot(both, sel[0 : lists * SUB, f * el : (f + 1) * el])
+            here = slot(f)
+            there = jnp.logical_and(here >= 4 * el, here < 4 * el + lists * SUB)
+            dest[f] = jnp.where(there, y[:rows] + y[rows:], dest[f])
 
     polar, azimuth = angles[0], angles[1]
     parts = (jnp.sin(polar), jnp.cos(polar), jnp.sin(azimuth), jnp.cos(azimuth))
@@ -192,8 +196,6 @@
         for i, row in enumerate((w * ca * cb, w * ca * sb, -w * sa, -w * sb, w * cb)):
             coef[f, i : i + 1, :] = row
         pool_store(f, own[f])
-        down = lax.broadcasted_iota(jnp.int32, (CHUNK, el), 0)
-        sel[:, f * el : (f + 1) * el] = jnp.where(down == slot(f) % CHUNK, 1.0, 0.0).astype(bf16)
     down = lax.broadcasted_iota(jnp.int32, (CHUNK, 3 * SUB), 0)
     sel_send[...] = jnp.where(down == send_list() % CHUNK, 1.0, 0.0).astype(bf16)
     remote[...] = jnp.zeros_like(remote)
@@ -205,6 +207,9 @@
     )
     start(0, has_prev, has_next, True)
 
+    for f in range(4):
+        down = lax.broadcasted_iota(jnp.int32, (CHUNK, el), 0)
+        sel[:, f * el : (f + 1) * el] = jnp.where(down == slot(f) % CHUNK, 1.0, 0.0).astype(bf16)
     gather_local(8, recv_n)
 
     fpad[...] = jnp.zeros_like(fpad)
@@ -303,17 +308,20 @@
             mask = jnp.where(kind[...] == k + 1, 1.0, 0.0).astype(bf16)
             return dot(weights[k], rhs[...] * mask)
 
+        for f in range(4):
+            base[f] = jnp.where(slot(f) >= 4 * el + 2 * SUB, ext[f], 0.0)
+
         def sweep(no, carry):
             right_side()
             tr[...] = blocks(wt, 0)
             for k in range(1, binv.shape[0]):
                 tr[...] += blocks(wt, k)
             fill_pool()
-            outgoing(no, 2 * FP)
+            outgoing(no, 2 * FP, 2)
             start(no, fine_prev, fine_next, False)
-            gather_local(2 * FP, ext)
+            gather_local(2 * FP, ext, base)
             finish(no, fine_prev, fine_next, False)
-            gather_remote(2 * FP, ext)
+            gather_remote(2 * FP, ext, 2)
             return carry
 
         lax.fori_loop(2, SWEEPS + 1, sweep, 0)
@@ -356,6 +364,7 @@
             vmem((3, 2 * FP, SUB), f32),
             vmem((4, 2 * FP, el), f32),
             vmem((2 * NC * RP, el), bf16),
+            vmem((4, 2 * FP, el), f32),
             vmem((SWEEPS + 1, 3, 2 * FP, SUB), f32),
             vmem((SWEEPS + 1, 3, 2 * FP, SUB), f32),
             pltpu.SemaphoreType.DMA((SWEEPS + 1, 3)),

time: 40.1 us -> 39.8 us (level)
  no operation moved by 1% of the time
where the time goes in v3:
time: 39.8 us; the launch traced here: 39.6 us
  Pallas kernels  37.3 us (94%)
  local copies, waits for them, and re-layouts  2.25 us (6%)
    pallas_call x1, Pallas kernels, shards(): pl.pallas_call(functools.partial(kernel, el), out_shape=jax.ShapeDtypeStr...  37.3 us
    unnamed x1, local copies, waits for them, and re-layouts  2.25 us

profile of v3, /device:TPU:23, one launch (start us, length us, event | category | flops | bytes accessed | tf_op | source)
XLA Modules:
  0.0 39.6 jit_solution(3715111580375423761)
XLA Ops:
  0.0 37.3 %shard_map.163 = f32[6,35,1024]{2,1,0:T(8,128)} custom-call(f32[6,35,1024]{2,1,0:T(8,128)} %fields.1, f32[9,1024]{1,0:T(8,128)} %metric.1, f32[4,1024]{1,0:T(4,128)} %scale.1, f32[2,4,1024]{2,1,0:T(4,128)} %angles.1, s32[4,1024]{1,0:T(4,128)} %nb.1, s32[2,128]{1,0:T(2,128)} %send_dom.1, s32[1,128]{1,0:T(1,128)} %bitcast.3, s32[1,1024]{1,0:T(1,128)} %bitcast.2, ...), custom_call_target="tpu_custom_call" | custom-call | tf_op jit(solution)/shard_map/pallas_call | solution.py:345
  37.4 2.2 %copy.19 = f32[6,35,1024]{2,1,0:T(8,128)} copy(f32[6,35,1024]{2,1,0:T(8,128)} %shard_map.163) | data formatting | bytes 1720320
